TPU v7x, 32 devices: a whole 2x2x4 slice. The times are simulated.
32 devices in a mesh: groups: 2 (over y), col: 16 (over z, x, core).
Axes of the slice: x: 2, y: 2, z: 4, core: 2. Of those that a mesh axis runs over, the one named last changes fastest.
Arguments:
- position: float32 [3, 8192], P(None, ('groups', 'col')), parts along dimension 1, may hold values from -6 to 6
- velocity: float32 [3, 8192], P(None, ('groups', 'col')), parts along dimension 1, may hold values from -6 to 6
- old_accel: float32 [3, 8192], P(None, ('groups', 'col')), parts along dimension 1, may hold values from -6 to 6
- old_jerk: float32 [3, 8192], P(None, ('groups', 'col')), parts along dimension 1, may hold values from -6 to 6
- mass: float32 [8192], P(('groups', 'col')), parts along dimension 0, may hold values from 7.324219e-05 to 0.0007324219
- elapsed: float32 [8192], P(('groups', 'col')), parts along dimension 0, may hold values from 0.125 to 1
- active_index: int32 [8192], P(('groups', 'col')), parts along dimension 0, may hold values from 0 to 255, as said below
- active_count: int32 [32], P(('groups', 'col')), parts along dimension 0, may hold values from 1 to 256, as said below
Outputs:
- new_state: float32 [6, 8192], P(None, ('groups', 'col')), parts along dimension 1
- new_deriv: float32 [6, 8192], P(None, ('groups', 'col')), parts along dimension 1
There are 2 independent parts, one for each index of `groups`. A program takes and returns all parts, laid end to end along the dimension named above; each array names one. Nothing has to cross between parts.
Inputs may be any that keep to these rules, and one draw needn't show every extreme that they name: `active_index`: within one device's slots all indices differ. `active_count`: some device has all 256 slots used in every draw.
All inputs are finite; a program needn't handle non-finite values.
Results may differ from a plain program's by a relative error of at most 0.00002.
Values sent between devices are 32-bit elements; how exact they have to be, the bound alone decides.
A program may use at most 64 MiB of HBM per device.

v0:
```python
import jax
import jax.numpy as jnp
from jax import lax
from jax.sharding import PartitionSpec as P

soften_sq = 0.01


def pair_block(targets, sources):
    tgt_pos = targets[0:3]
    tgt_vel = targets[3:6]
    offset = sources[0:3][:, None, :] - tgt_pos[:, :, None]
    relvel = sources[3:6][:, None, :] - tgt_vel[:, :, None]
    dist_sq = jnp.sum(offset * offset, axis=0) + soften_sq
    inv_dist = lax.rsqrt(dist_sq)
    strength = sources[6][None, :] * inv_dist * inv_dist * inv_dist
    along = jnp.sum(offset * relvel, axis=0) / dist_sq
    new_accel = jnp.sum(strength[None] * offset, axis=-1)
    new_jerk = jnp.sum(strength[None] * (relvel - 3.0 * along[None] * offset), axis=-1)
    return jnp.concatenate([new_accel, new_jerk], axis=0)


def over_sources(targets, sources):
    count = sources.shape[1]
    pieces = sources.reshape(7, count // 1024, 1024).transpose(1, 0, 2)

    def add_piece(total, piece):
        return (total + pair_block(targets, piece), None)

    start_sum = jnp.zeros((6, targets.shape[1]), jnp.float32)
    result, _ = lax.scan(add_piece, start_sum, pieces)
    return result


def pair_forces(targets, sources):
    return over_sources(targets, sources)


def body(position, velocity, old_accel, old_jerk, mass, elapsed, active_index, active_count):
    span = elapsed[None, :]
    pred_pos = (
        position
        + span * velocity
        + span * span / 2.0 * old_accel
        + span * span * span / 6.0 * old_jerk
    )
    pred_vel = velocity + span * old_accel + span * span / 2.0 * old_jerk
    sources = jnp.concatenate([pred_pos, pred_vel, mass[None, :]], axis=0)
    targets = jnp.concatenate([pred_pos[:, active_index], pred_vel[:, active_index]], axis=0)
    derivs = pair_forces(targets, lax.all_gather(sources, "col", axis=1, tiled=True))
    new_accel = derivs[0:3]
    new_jerk = derivs[3:6]
    step_len = elapsed[active_index][None, :]
    x_old = position[:, active_index]
    v_old = velocity[:, active_index]
    a_old = old_accel[:, active_index]
    j_old = old_jerk[:, active_index]
    v_new = (
        v_old
        + step_len / 2.0 * (a_old + new_accel)
        + step_len * step_len / 12.0 * (j_old - new_jerk)
    )
    x_new = (
        x_old + step_len / 2.0 * (v_old + v_new) + step_len * step_len / 12.0 * (a_old - new_accel)
    )
    slot_ids = jnp.arange(targets.shape[1], dtype=jnp.int32)
    used = slot_ids < active_count[0]
    state = jnp.concatenate([x_new, v_new], axis=0)
    new_state = jnp.where(used[None, :], state, jnp.zeros_like(state))
    new_deriv = jnp.where(used[None, :], derivs, jnp.zeros_like(derivs))
    return (new_state, new_deriv)


def solution(mesh):
    placed = (
        P(None, ("groups", "col")),
        P(None, ("groups", "col")),
        P(None, ("groups", "col")),
        P(None, ("groups", "col")),
        P(("groups", "col")),
        P(("groups", "col")),
        P(("groups", "col")),
        P(("groups", "col")),
    )
    return jax.shard_map(
        body,
        mesh=mesh,
        in_specs=placed,
        out_specs=(P(None, ("groups", "col")), P(None, ("groups", "col"))),
        check_vma=False,
    )
```

profile of v0, /device:TPU:0, one launch (start us, length us, event | category | flops | bytes accessed | tf_op | source)
XLA Modules:
  0.0 45.6 jit_solution(2330704366039589943)
XLA Ops:
  0.6 0.7 %compare_select_fusion = s32[256]{0:T(256)S(1)} fusion(s32[256]{0:T(256)} %param.16), kind=kLoop, calls=%fused_computation.41 | loop fusion | flops 768 | bytes 2048 | tf_op jit(solution)/shard_map/select_n | solution.py:54
  1.3 0.7 %fusion.13 = (f32[256]{0:T(256)S(1)}, f32[256]{0:T(256)S(1)}) fusion(f32[256]{0:T(256)} %param.15), kind=kLoop, calls=%fused_computation.44 | loop fusion | flops 1024 | bytes 3072 | tf_op jit(solution)/shard_map/div | solution.py:45
  2.0 0.8 %multiply_add_fusion.1 = (f32[3,256]{1,0:T(4,128)S(1)}, f32[3,256]{1,0:T(4,128)S(1)}) fusion(f32[3,256]{1,0:T(4,128)} %param.13, f32[3,256]{1,0:T(4,128)} %param.12, f32[3,256]{1,0:T(4,128)} %param.10, f32[3,256]{1,0:T(4,128)} %param.11, f32[256]{0:T(256)S(1)} %get-tuple-element.101, f32[256]{0:T(256)S(1)} %get-tuple-element.102, f32[256]{0:T(256)} %param.15), kind=kLoop, calls=%fused_computation.39 | loop fusion | flops 7680 | bytes 21504 | tf_op jit(solution)/shard_map/add | solution.py:42
  2.8 0.1 copy.122
  2.9 0.7 %gather_fusion.4 = f32[256,3]{1,0:T(8,128)S(1)} fusion(f32[3,256]{0,1:T(8,128)S(1)} %copy.122, s32[1024]{0:T(1024)S(1)} %pad_clamp_fusion), kind=kCustom, calls=%fused_computation.4 | custom fusion | bytes 7168 | tf_op jit(solution)/shard_map/gather | solution.py:49
  3.7 0.1 copy.123
  3.9 0.7 %gather_fusion.5 = f32[256,3]{1,0:T(8,128)S(1)} fusion(f32[3,256]{0,1:T(8,128)S(1)} %copy.123, s32[1024]{0:T(1024)S(1)} %pad_clamp_fusion), kind=kCustom, calls=%fused_computation.5 | custom fusion | bytes 7168 | tf_op jit(solution)/shard_map/gather | solution.py:49
  4.7 0.7 %pad_maximum_fusion = f32[7,256]{1,0:T(8,128)S(1)} fusion(f32[1,256]{1,0:T(1,128)} %bitcast.54, f32[3,256]{1,0:T(4,128)S(1)} %get-tuple-element.98, f32[3,256]{1,0:T(4,128)S(1)} %get-tuple-element.97), kind=kLoop, calls=%fused_computation.23 | loop fusion | flops 3584 | bytes 14336 | tf_op jit(solution)/shard_map/concatenate | solution.py:48
  5.4 23.4 %all_gather.3 = f32[7,4096]{1,0:T(8,128)S(1)} all-gather(f32[7,256]{1,0:T(8,128)S(1)} %pad_maximum_fusion), channel_id=1, replica_groups=mesh['groups'=2,'col'=16] {'col'}, dimensions={1}, use_global_device_ids=true | all-gather | bytes 121856 | tf_op jit(solution)/shard_map/all_gather | solution.py:50
  28.8 9.7 %while.11 = (s32[]{:T(128)}, f32[6,256]{1,0:T(8,128)S(1)}, f32[4,7,1024]{2,1,0:T(8,128)S(1)}, f32[3,256]{1,0:T(4,128)S(1)}, f32[3,256]{1,0:T(4,128)S(1)}, /*index=5*/s32[]{:T(128)}, s32[]{:T(128)}, s32[]{}, s32[]{}) while((s32[]{:T(128)}, f32[6,256]{1,0:T(8,128)S(1)}, f32[4,7,1024]{2,1,0:T(8,128)S(1)}, f32[3,256]{1,0:T(4,128)S(1)}, ...), condition=%wide.region_5.6_spmd.clone, body=%wide.region_0.5_spmd.clone.sunk | while | flops 12061701 | bytes 8536207 | solution.py:31
  28.8 0.7 %fusion.17 = (f32[256,1024]{1,0:T(8,128)S(1)}, f32[256,1024]{1,0:T(8,128)S(1)}) fusion(f32[3,256]{1,0:T(4,128)S(1)} %get-tuple-element.173, f32[3,1024]{1,0:T(4,128)S(1)} %get-tuple-element.144, f32[3,256]{1,0:T(4,128)S(1)} %get-tuple-element.174, f32[3,1024]{1,0:T(4,128)S(1)} %get-tuple-element.145), kind=kLoop, calls=%fused_computation.14.clone.1 | loop fusion | flops 4194304 | bytes 2127872 | tf_op jit(solution)/shard_map/while/body/eval_jaxpr/reduce_sum | solution.py:14
  29.5 0.3 divide_multiply_fusion.2
  29.8 1.4 %fusion.18 = (f32[3,256]{1,0:T(4,128)S(1)}, f32[3,256]{1,0:T(4,128)S(1)}) fusion(f32[256,1024]{1,0:T(8,128)S(1)} %get-tuple-element.148, f32[3,256]{1,0:T(4,128)S(1)} %get-tuple-element.173, f32[3,1024]{1,0:T(4,128)S(1)} %get-tuple-element.144, f32[256,1024]{1,0:T(8,128)S(1)} %get-tuple-element.149, f32[3,256]{1,0:T(4,128)S(1)} %get-tuple-element.174, ...), kind=kLoop, calls=%fused_computation.15.clone.1 | loop fusion | flops 6289920 | bytes 2134016 | tf_op jit(solution)/shard_map/while/body/eval_jaxpr/reduce_sum | solution.py:18
  31.2 0.7 %fusion.17 = (f32[256,1024]{1,0:T(8,128)S(1)}, f32[256,1024]{1,0:T(8,128)S(1)}) fusion(f32[3,256]{1,0:T(4,128)S(1)} %get-tuple-element.173, f32[3,1024]{1,0:T(4,128)S(1)} %get-tuple-element.144, f32[3,256]{1,0:T(4,128)S(1)} %get-tuple-element.174, f32[3,1024]{1,0:T(4,128)S(1)} %get-tuple-element.145), kind=kLoop, calls=%fused_computation.14.clone.1 | loop fusion | flops 4194304 | bytes 2127872 | tf_op jit(solution)/shard_map/while/body/eval_jaxpr/reduce_sum | solution.py:14
  31.9 0.3 divide_multiply_fusion.2
  32.2 1.4 %fusion.18 = (f32[3,256]{1,0:T(4,128)S(1)}, f32[3,256]{1,0:T(4,128)S(1)}) fusion(f32[256,1024]{1,0:T(8,128)S(1)} %get-tuple-element.148, f32[3,256]{1,0:T(4,128)S(1)} %get-tuple-element.173, f32[3,1024]{1,0:T(4,128)S(1)} %get-tuple-element.144, f32[256,1024]{1,0:T(8,128)S(1)} %get-tuple-element.149, f32[3,256]{1,0:T(4,128)S(1)} %get-tuple-element.174, ...), kind=kLoop, calls=%fused_computation.15.clone.1 | loop fusion | flops 6289920 | bytes 2134016 | tf_op jit(solution)/shard_map/while/body/eval_jaxpr/reduce_sum | solution.py:18
  33.6 0.7 %fusion.17 = (f32[256,1024]{1,0:T(8,128)S(1)}, f32[256,1024]{1,0:T(8,128)S(1)}) fusion(f32[3,256]{1,0:T(4,128)S(1)} %get-tuple-element.173, f32[3,1024]{1,0:T(4,128)S(1)} %get-tuple-element.144, f32[3,256]{1,0:T(4,128)S(1)} %get-tuple-element.174, f32[3,1024]{1,0:T(4,128)S(1)} %get-tuple-element.145), kind=kLoop, calls=%fused_computation.14.clone.1 | loop fusion | flops 4194304 | bytes 2127872 | tf_op jit(solution)/shard_map/while/body/eval_jaxpr/reduce_sum | solution.py:14
  34.4 0.3 divide_multiply_fusion.2
  34.6 1.4 %fusion.18 = (f32[3,256]{1,0:T(4,128)S(1)}, f32[3,256]{1,0:T(4,128)S(1)}) fusion(f32[256,1024]{1,0:T(8,128)S(1)} %get-tuple-element.148, f32[3,256]{1,0:T(4,128)S(1)} %get-tuple-element.173, f32[3,1024]{1,0:T(4,128)S(1)} %get-tuple-element.144, f32[256,1024]{1,0:T(8,128)S(1)} %get-tuple-element.149, f32[3,256]{1,0:T(4,128)S(1)} %get-tuple-element.174, ...), kind=kLoop, calls=%fused_computation.15.clone.1 | loop fusion | flops 6289920 | bytes 2134016 | tf_op jit(solution)/shard_map/while/body/eval_jaxpr/reduce_sum | solution.py:18
  36.1 0.7 %fusion.17 = (f32[256,1024]{1,0:T(8,128)S(1)}, f32[256,1024]{1,0:T(8,128)S(1)}) fusion(f32[3,256]{1,0:T(4,128)S(1)} %get-tuple-element.173, f32[3,1024]{1,0:T(4,128)S(1)} %get-tuple-element.144, f32[3,256]{1,0:T(4,128)S(1)} %get-tuple-element.174, f32[3,1024]{1,0:T(4,128)S(1)} %get-tuple-element.145), kind=kLoop, calls=%fused_computation.14.clone.1 | loop fusion | flops 4194304 | bytes 2127872 | tf_op jit(solution)/shard_map/while/body/eval_jaxpr/reduce_sum | solution.py:14
  36.8 0.3 divide_multiply_fusion.2
  37.1 1.4 %fusion.18 = (f32[3,256]{1,0:T(4,128)S(1)}, f32[3,256]{1,0:T(4,128)S(1)}) fusion(f32[256,1024]{1,0:T(8,128)S(1)} %get-tuple-element.148, f32[3,256]{1,0:T(4,128)S(1)} %get-tuple-element.173, f32[3,1024]{1,0:T(4,128)S(1)} %get-tuple-element.144, f32[256,1024]{1,0:T(8,128)S(1)} %get-tuple-element.149, f32[3,256]{1,0:T(4,128)S(1)} %get-tuple-element.174, ...), kind=kLoop, calls=%fused_computation.15.clone.1 | loop fusion | flops 6289920 | bytes 2134016 | tf_op jit(solution)/shard_map/while/body/eval_jaxpr/reduce_sum | solution.py:18
  38.5 1.9 %gather_fusion.1 = f32[256]{0:T(256)S(1)} fusion(f32[256]{0:T(256)S(1)} %copy-done, s32[1024]{0:T(1024)S(1)} %pad_clamp_fusion), kind=kCustom, calls=%fused_computation.1 | custom fusion | bytes 3072 | tf_op jit(solution)/shard_map/gather | solution.py:53
  40.5 0.1 copy.115
  40.6 0.7 %gather_fusion = f32[256,3]{1,0:T(8,128)S(1)} fusion(f32[3,256]{0,1:T(8,128)S(1)} %copy.115, s32[1024]{0:T(1024)S(1)} %pad_clamp_fusion), kind=kCustom, calls=%fused_computation | custom fusion | bytes 7168 | tf_op jit(solution)/shard_map/gather | solution.py:54
  41.4 0.1 copy.117
  41.6 0.7 %gather_fusion.2 = f32[256,3]{1,0:T(8,128)S(1)} fusion(f32[3,256]{0,1:T(8,128)S(1)} %copy.117, s32[1024]{0:T(1024)S(1)} %pad_clamp_fusion), kind=kCustom, calls=%fused_computation.2 | custom fusion | bytes 7168 | tf_op jit(solution)/shard_map/gather | solution.py:55
  42.4 0.1 copy.119
  42.6 0.7 %gather_fusion.3 = f32[256,3]{1,0:T(8,128)S(1)} fusion(f32[3,256]{0,1:T(8,128)S(1)} %copy.119, s32[1024]{0:T(1024)S(1)} %pad_clamp_fusion), kind=kCustom, calls=%fused_computation.3 | custom fusion | bytes 7168 | tf_op jit(solution)/shard_map/gather | solution.py:56
  43.4 0.1 copy.126
  43.5 0.7 %gather_fusion.6 = f32[256,3]{1,0:T(8,128)S(1)} fusion(f32[3,256]{0,1:T(8,128)S(1)} %copy.126, s32[1024]{0:T(1024)S(1)} %pad_clamp_fusion), kind=kCustom, calls=%fused_computation.6 | custom fusion | bytes 7168 | tf_op jit(solution)/shard_map/gather | solution.py:57
  45.0 0.6 %broadcast_select_fusion = (f32[6,256]{1,0:T(8,128)}, f32[6,256]{1,0:T(8,128)}) fusion(f32[6,256]{1,0:T(8,128)S(1)} %get-tuple-element.29, pred[256]{0:T(512)(128)(4,1)S(1)} %iota_compare_fusion, f32[3,256]{1,0:T(4,128)S(1)} %get-tuple-element.92, f32[3,256]{1,0:T(4,128)S(1)} %get-tuple-element.91), kind=kLoop, calls=%fused_computation.40 | loop fusion | flops 4608 | bytes 24832 | tf_op jit(solution)/shard_map/jit(_where)/select_n | solution.py:70
  (33 shorter events, 0.7 us)
Async XLA Ops:
  28.8 9.7 %copy-start = (f32[256]{0:T(256)S(1)}, f32[256]{0:T(256)}, u32[]{:S(2)}) copy-start(f32[256]{0:T(256)} %param.15) | copy-start | bytes 3076
  38.5 2.0 %copy-start.1 = (f32[3,256]{1,0:T(4,128)S(1)}, f32[3,256]{1,0:T(4,128)}, u32[]{:S(2)}) copy-start(f32[3,256]{1,0:T(4,128)} %param.10) | copy-start | bytes 9220
  38.5 3.0 %copy-start.2 = (f32[3,256]{1,0:T(4,128)S(1)}, f32[3,256]{1,0:T(4,128)}, u32[]{:S(2)}) copy-start(f32[3,256]{1,0:T(4,128)} %param.11) | copy-start | bytes 9220
  38.5 3.9 %copy-start.3 = (f32[3,256]{1,0:T(4,128)S(1)}, f32[3,256]{1,0:T(4,128)}, u32[]{:S(2)}) copy-start(f32[3,256]{1,0:T(4,128)} %param.12) | copy-start | bytes 9220
  38.5 4.9 %copy-start.4 = (f32[3,256]{1,0:T(4,128)S(1)}, f32[3,256]{1,0:T(4,128)}, u32[]{:S(2)}) copy-start(f32[3,256]{1,0:T(4,128)} %param.13) | copy-start | bytes 9220
where the time goes:
time: 45.9 us; the launch traced here: 45.6 us
  blocking collectives  23.4 us (51%)
  other arithmetic  12.8 us (28%)
  local copies, waits for them, and re-layouts  7.78 us (17%)
  between operations  1.42 us (3%)
    all_gather x1, blocking collectives, body(): lax.all_gather(sources, 'col', axis=1, tiled=True)  23.4 us
    reduce_sum x4, other arithmetic, pair_block(): new_accel = jnp.sum(strength[None] * offset, axis=-1)  5.46 us
    reduce_sum x4, other arithmetic, pair_block(): dist_sq = jnp.sum(offset * offset, axis=0) + soften_sq  2.74 us
    gather x1, local copies, waits for them, and re-layouts, body(): step_len = elapsed[active_index][None, :]  1.94 us
    mul x4, other arithmetic, pair_block(): 3.0 * along[None] * offset  1.13 us

commit v1 on v0

v1 whole, which is shorter than its diff:
```python
import functools

import jax
import jax.numpy as jnp
from jax import lax
from jax.experimental import pallas as pl
from jax.experimental.pallas import tpu as pltpu
from jax.sharding import PartitionSpec as P

soften_sq = 0.01
LANES = 128
SUBLANES = 8
UNROLL = 8


def predict(x, v, a, j, t):
    pos = x + t * v + t * t / 2.0 * a + t * t * t / 6.0 * j
    vel = v + t * a + t * t / 2.0 * j
    return pos, vel


def pick(rows, index):
    width, slots = rows.shape[1], index.shape[1]
    outs = []
    for s in range(0, slots, LANES):
        idx = index[:, s : s + LANES]
        got = None
        for w in range(0, width, LANES):
            local = jnp.bitwise_and(idx, LANES - 1)
            piece = jnp.take_along_axis(
                rows[:, w : w + LANES], local, axis=1, mode="promise_in_bounds"
            )
            got = piece if got is None else jnp.where(idx >= w, piece, got)
        outs.append(got)
    return jnp.concatenate(outs, axis=1)


def kernel(
    n,
    pos_ref, vel_ref, acc_ref, jrk_ref, mass_ref, span_ref, index_ref, count_ref,
    state_ref, deriv_ref,
    field, raw, targets, total, send_sem, recv_sem,
):
    me = lax.axis_index("col")
    slots = index_ref.shape[1]
    width = mass_ref.shape[1]
    groups = slots // SUBLANES

    barrier = pltpu.get_barrier_semaphore()

    def greet(k, _):
        pl.semaphore_signal(
            barrier, inc=1, device_id={"col": lax.rem(me + k, n)},
            device_id_type=pl.DeviceIdType.MESH,
        )
        return 0

    lax.fori_loop(1, n, greet, 0)

    span = span_ref[...]
    pos, vel = predict(pos_ref[...], vel_ref[...], acc_ref[...], jrk_ref[...], span)
    field[me, 0:3] = pos
    field[me, 3:6] = vel
    field[me, 6:7] = mass_ref[...]
    field[me, 7:8] = mass_ref[...]

    pl.semaphore_wait(barrier, n - 1)

    def copy_to(k):
        peer = lax.rem(me + k, n)
        return pltpu.make_async_remote_copy(
            src_ref=field.at[me],
            dst_ref=field.at[me],
            send_sem=send_sem.at[peer],
            recv_sem=recv_sem.at[me],
            device_id={"col": peer},
            device_id_type=pl.DeviceIdType.MESH,
        )

    def send(k, _):
        copy_to(k).start()
        return 0

    lax.fori_loop(1, n, send, 0)

    raw[0:3] = pos_ref[...]
    raw[3:6] = vel_ref[...]
    raw[6:8] = jnp.zeros((2, width), jnp.float32)
    raw[8:11] = acc_ref[...]
    raw[11:14] = jrk_ref[...]
    raw[14:15] = span
    raw[15:16] = span
    index = jnp.broadcast_to(index_ref[...], (SUBLANES, slots))
    first = pick(raw[0:8], index)
    second = pick(raw[8:16], index)
    x0, v0 = first[0:3], first[3:6]
    a0, j0, dt = second[0:3], second[3:6], second[6:7]
    tpos, tvel = predict(x0, v0, a0, j0, dt)
    tcols = jnp.concatenate(
        [tpos, tvel, jnp.zeros((2, slots), jnp.float32)], axis=0
    ).T
    for c in range(6):
        targets[c] = jnp.broadcast_to(tcols[:, c : c + 1], (slots, LANES))
        total[c] = jnp.zeros((slots, LANES), jnp.float32)

    def add_block(b):
        for w in range(0, width, 2 * LANES):
            srcs = [
                [
                    jnp.broadcast_to(
                        field[b, c : c + 1, w + h : w + h + LANES], (SUBLANES, LANES)
                    )
                    for c in range(7)
                ]
                for h in range(0, min(2 * LANES, width - w), LANES)
            ]

            def add_groups(g, _):
                for u in range(UNROLL):
                    at = pl.ds(pl.multiple_of((g * UNROLL + u) * SUBLANES, SUBLANES), SUBLANES)
                    tgt = [targets[c, at] for c in range(6)]
                    sums = [total[c, at] for c in range(6)]
                    for src in srcs:
                        dx = [src[c] - tgt[c] for c in range(3)]
                        dv = [src[c + 3] - tgt[c + 3] for c in range(3)]
                        dist_sq = dx[0] * dx[0] + dx[1] * dx[1] + dx[2] * dx[2] + soften_sq
                        inv = lax.rsqrt(dist_sq)
                        inv_sq = inv * inv
                        strength = src[6] * inv * inv_sq
                        dot = dx[0] * dv[0] + dx[1] * dv[1] + dx[2] * dv[2]
                        along = 3.0 * dot * inv_sq
                        for c in range(3):
                            pull = strength * dx[c]
                            sums[c] = sums[c] + pull
                            sums[c + 3] = sums[c + 3] + (strength * dv[c] - along * pull)
                    for c in range(6):
                        total[c, at] = sums[c]
                return 0

            lax.fori_loop(0, groups // UNROLL, add_groups, 0)

    add_block(me)

    def arrive(k, _):
        b = lax.rem(me + n - k, n)
        pltpu.make_async_remote_copy(
            src_ref=field.at[b],
            dst_ref=field.at[b],
            send_sem=send_sem.at[b],
            recv_sem=recv_sem.at[b],
            device_id={"col": b},
            device_id_type=pl.DeviceIdType.MESH,
        ).wait_recv()
        add_block(b)
        return 0

    lax.fori_loop(1, n, arrive, 0)

    rows = [jnp.sum(total[c].T, axis=0, keepdims=True) for c in range(6)]
    new_acc = jnp.concatenate(rows[0:3], axis=0)
    new_jrk = jnp.concatenate(rows[3:6], axis=0)
    v1 = v0 + dt / 2.0 * (a0 + new_acc) + dt * dt / 12.0 * (j0 - new_jrk)
    x1 = x0 + dt / 2.0 * (v0 + v1) + dt * dt / 12.0 * (a0 - new_acc)
    used = lax.broadcasted_iota(jnp.int32, (3, slots), 1) < count_ref[...]
    state_ref[0:3] = jnp.where(used, x1, 0.0)
    state_ref[3:6] = jnp.where(used, v1, 0.0)
    deriv_ref[0:3] = jnp.where(used, new_acc, 0.0)
    deriv_ref[3:6] = jnp.where(used, new_jrk, 0.0)

    def sent(k, _):
        copy_to(k).wait_send()
        return 0

    lax.fori_loop(1, n, sent, 0)


def solution(mesh):
    n = mesh.shape["col"]

    def body(position, velocity, old_accel, old_jerk, mass, elapsed, active_index, active_count):
        width, slots = mass.shape[0], active_index.shape[0]
        out = jax.ShapeDtypeStruct((6, slots), jnp.float32)
        return pl.pallas_call(
            functools.partial(kernel, n),
            out_shape=(out, out),
            in_specs=[pl.BlockSpec(memory_space=pltpu.VMEM)] * 8,
            out_specs=(pl.BlockSpec(memory_space=pltpu.VMEM),) * 2,
            scratch_shapes=[
                pltpu.VMEM((n, 8, width), jnp.float32),
                pltpu.VMEM((16, width), jnp.float32),
                pltpu.VMEM((6, slots, LANES), jnp.float32),
                pltpu.VMEM((6, slots, LANES), jnp.float32),
                pltpu.SemaphoreType.DMA((n,)),
                pltpu.SemaphoreType.DMA((n,)),
            ],
            compiler_params=pltpu.CompilerParams(
                collective_id=0, has_side_effects=True, vmem_limit_bytes=16 << 20
            ),
        )(
            position, velocity, old_accel, old_jerk,
            mass[None, :], elapsed[None, :], active_index[None, :], active_count[None, :],
        )

    wide, flat = P(None, ("groups", "col")), P(("groups", "col"))
    return jax.shard_map(
        body,
        mesh=mesh,
        in_specs=(wide,) * 4 + (flat,) * 4,
        out_specs=(wide, wide),
        check_vma=False,
    )
```

time: 45.9 us -> 20.7 us (0.45)
  blocking collectives: 23.4 us -> 0 us
  Pallas kernels: 0 us -> 14.4 us
  other arithmetic: 12.8 us -> 0 us
  local copies, waits for them, and re-layouts: 7.78 us -> 4.6 us
    all_gather x1 -> x0, blocking collectives: 23.4 us -> none  [body(): lax.all_gather(sources, 'col', axis=1, tiled=True)]
    pallas_call x0 -> x1, Pallas kernels: none -> 14.4 us  [body(): pl.pallas_call(functools.partial(kernel, n), out_shape=(out, out), in_spe...]
    reduce_sum x8 -> x0, other arithmetic: 8.2 us -> none  [the longest x4 5.46 us: pair_block(): new_accel = jnp.sum(strength[None] * offset, axis=-1)]
    gather x11 -> x0, local copies, waits for them, and re-layouts: 6.65 us -> none  [the longest x1 1.94 us: body(): step_len = elapsed[active_index][None, :]]
    unnamed x16, local copies, waits for them, and re-layouts: 0.75 us -> 4.6 us
    select_n x2 -> x0, other arithmetic: 1.29 us -> none  [the longest x1 0.68 us: body(): x_old = position[:, active_index]]
    mul x4 -> x0, other arithmetic: 1.13 us -> none  [pair_block(): 3.0 * along[None] * offset]
    add x6 -> x0, other arithmetic: 0.82 us -> none  [the longest x1 0.75 us: body(): position + span * velocity + span * span / 2.0 * old_accel]
where the time goes in v1:
time: 20.7 us; the launch traced here: 20.4 us
  Pallas kernels  14.4 us (70%)
  local copies, waits for them, and re-layouts  4.6 us (22%)
  between operations  1.34 us (6%)
    pallas_call x1, Pallas kernels, body(): pl.pallas_call(functools.partial(kernel, n), out_shape=(out, out), in_spe...  14.4 us
    unnamed x16, local copies, waits for them, and re-layouts  4.6 us

profile of v1, /device:TPU:0, one launch (start us, length us, event | category | flops | bytes accessed | tf_op | source)
XLA Modules:
  0.0 20.4 jit_solution(17236370533286265772)
XLA Ops:
  0.6 0.0 copy-start.1
  1.3 0.0 copy-start
  1.3 0.0 copy-start.4
  1.3 0.0 copy-done.1
  1.3 0.7 %copy-done = f32[3,256]{1,0:T(4,128)S(1)} copy-done((f32[3,256]{1,0:T(4,128)S(1)}, f32[3,256]{1,0:T(4,128)}, u32[]{:S(2)}) %copy-start) | copy-done | bytes 3096
  2.0 0.0 copy-done.4
  2.0 0.0 copy-start.2
  2.0 0.7 %copy-done.2 = f32[3,256]{1,0:T(4,128)S(1)} copy-done((f32[3,256]{1,0:T(4,128)S(1)}, f32[3,256]{1,0:T(4,128)}, u32[]{:S(2)}) %copy-start.2) | copy-done | bytes 3096
  2.7 0.0 copy-start.3
  2.7 0.7 %copy-done.3 = f32[3,256]{1,0:T(4,128)S(1)} copy-done((f32[3,256]{1,0:T(4,128)S(1)}, f32[3,256]{1,0:T(4,128)}, u32[]{:S(2)}) %copy-start.3) | copy-done | bytes 3096
  3.4 0.0 copy-start.5
  3.4 0.7 %copy-done.5 = f32[256]{0:T(256)S(1)} copy-done((f32[256]{0:T(256)S(1)}, f32[256]{0:T(256)}, u32[]{:S(2)}) %copy-start.5) | copy-done | bytes 1048
  4.1 0.0 copy-start.6
  4.1 0.7 %copy-done.6 = s32[256]{0:T(256)S(1)} copy-done((s32[256]{0:T(256)S(1)}, s32[256]{0:T(256)}, u32[]{:S(2)}) %copy-start.6) | copy-done | bytes 1048
  4.7 14.4 %shard_map.95 = (f32[6,256]{1,0:T(8,128)S(1)}, f32[6,256]{1,0:T(8,128)S(1)}) custom-call(f32[3,256]{1,0:T(4,128)S(1)} %copy-done, f32[3,256]{1,0:T(4,128)S(1)} %copy-done.1, f32[3,256]{1,0:T(4,128)S(1)} %copy-done.2, f32[3,256]{1,0:T(4,128)S(1)} %copy-done.3, f32[1,256]{1,0:T(1,128)S(1)} %bitcast.5, f32[1,256]{1,0:T(1,128)S(1)} %bitcast.6, ...), custom_call_target="tpu_custom_call" | custom-call | tf_op jit(solution)/shard_map/pallas_call | solution.py:183
  19.2 0.6 %copy.13 = f32[6,256]{1,0:T(8,128)} copy(f32[6,256]{1,0:T(8,128)S(1)} %get-tuple-element.4) | data formatting | bytes 12288
  19.8 0.6 %copy.14 = f32[6,256]{1,0:T(8,128)} copy(f32[6,256]{1,0:T(8,128)S(1)} %get-tuple-element.5) | data formatting | bytes 12288
Async XLA Ops:
  0.6 0.7 %copy-start.1 = (f32[3,256]{1,0:T(4,128)S(1)}, f32[3,256]{1,0:T(4,128)}, u32[]{:S(2)}) copy-start(f32[3,256]{1,0:T(4,128)} %vel_ref.1) | copy-start | bytes 9220
  1.3 0.7 %copy-start = (f32[3,256]{1,0:T(4,128)S(1)}, f32[3,256]{1,0:T(4,128)}, u32[]{:S(2)}) copy-start(f32[3,256]{1,0:T(4,128)} %pos_ref.1) | copy-start | bytes 9220
  1.3 0.7 %copy-start.4 = (f32[256]{0:T(256)S(1)}, f32[256]{0:T(256)}, u32[]{:S(2)}) copy-start(f32[256]{0:T(256)} %param.12) | copy-start | bytes 3076
  2.0 0.7 %copy-start.2 = (f32[3,256]{1,0:T(4,128)S(1)}, f32[3,256]{1,0:T(4,128)}, u32[]{:S(2)}) copy-start(f32[3,256]{1,0:T(4,128)} %acc_ref.1) | copy-start | bytes 9220
  2.7 0.7 %copy-start.3 = (f32[3,256]{1,0:T(4,128)S(1)}, f32[3,256]{1,0:T(4,128)}, u32[]{:S(2)}) copy-start(f32[3,256]{1,0:T(4,128)} %jrk_ref.1) | copy-start | bytes 9220
  3.4 0.7 %copy-start.5 = (f32[256]{0:T(256)S(1)}, f32[256]{0:T(256)}, u32[]{:S(2)}) copy-start(f32[256]{0:T(256)} %param.13) | copy-start | bytes 3076
  4.1 0.7 %copy-start.6 = (s32[256]{0:T(256)S(1)}, s32[256]{0:T(256)}, u32[]{:S(2)}) copy-start(s32[256]{0:T(256)} %param.14) | copy-start | bytes 3076

commit v2 on v1

--- a/solution.py
+++ b/solution.py
@@ -10,7 +10,7 @@
 soften_sq = 0.01
 LANES = 128
 SUBLANES = 8
-UNROLL = 8
+UNROLL = 16
 
 
 def predict(x, v, a, j, t):
@@ -35,27 +35,65 @@
     return jnp.concatenate(outs, axis=1)
 
 
+def partner(me, k, n):
+    if n & (n - 1):
+        return lax.rem(me + k, n), lax.rem(me + n - k, n)
+    other, bit = 0, 1
+    while bit < n:
+        other = other + lax.rem(lax.div(me, bit) + lax.div(jnp.int32(k), bit), 2) * bit
+        bit *= 2
+    return other, other
+
+
+def each(n, step):
+    if n <= 32:
+        for k in range(1, n):
+            step(k)
+        return
+
+    def one(k, _):
+        step(k)
+        return 0
+
+    lax.fori_loop(1, n, one, 0)
+
+
 def kernel(
     n,
+    pos_hbm, vel_hbm, acc_hbm, jrk_hbm, mass_hbm, span_hbm, index_hbm, count_hbm,
+    out_ref,
     pos_ref, vel_ref, acc_ref, jrk_ref, mass_ref, span_ref, index_ref, count_ref,
-    state_ref, deriv_ref,
-    field, raw, targets, total, send_sem, recv_sem,
+    field, raw, targets, total, send_sem, recv_sem, load_sem,
 ):
     me = lax.axis_index("col")
     slots = index_ref.shape[1]
+    loads = [
+        pltpu.make_async_copy(src, dst, load_sem.at[i])
+        for i, (src, dst) in enumerate(
+            (
+                (pos_hbm, pos_ref), (vel_hbm, vel_ref), (acc_hbm, acc_ref),
+                (jrk_hbm, jrk_ref), (span_hbm, span_ref), (mass_hbm, mass_ref),
+                (index_hbm, index_ref), (count_hbm, count_ref),
+            )
+        )
+    ]
+    for load in loads:
+        load.start()
     width = mass_ref.shape[1]
     groups = slots // SUBLANES
 
     barrier = pltpu.get_barrier_semaphore()
 
-    def greet(k, _):
+    def greet(k):
         pl.semaphore_signal(
-            barrier, inc=1, device_id={"col": lax.rem(me + k, n)},
+            barrier, inc=1, device_id={"col": partner(me, k, n)[0]},
             device_id_type=pl.DeviceIdType.MESH,
         )
-        return 0
-
-    lax.fori_loop(1, n, greet, 0)
+
+    each(n, greet)
+
+    for load in loads:
+        load.wait()
 
     span = span_ref[...]
     pos, vel = predict(pos_ref[...], vel_ref[...], acc_ref[...], jrk_ref[...], span)
@@ -67,7 +105,7 @@
     pl.semaphore_wait(barrier, n - 1)
 
     def copy_to(k):
-        peer = lax.rem(me + k, n)
+        peer = partner(me, k, n)[0]
         return pltpu.make_async_remote_copy(
             src_ref=field.at[me],
             dst_ref=field.at[me],
@@ -77,11 +115,10 @@
             device_id_type=pl.DeviceIdType.MESH,
         )
 
-    def send(k, _):
+    def send(k):
         copy_to(k).start()
-        return 0
-
-    lax.fori_loop(1, n, send, 0)
+
+    each(n, send)
 
     raw[0:3] = pos_ref[...]
     raw[3:6] = vel_ref[...]
@@ -142,7 +179,7 @@
     add_block(me)
 
     def arrive(k, _):
-        b = lax.rem(me + n - k, n)
+        b = partner(me, k, n)[1]
         pltpu.make_async_remote_copy(
             src_ref=field.at[b],
             dst_ref=field.at[b],
@@ -161,17 +198,16 @@
     new_jrk = jnp.concatenate(rows[3:6], axis=0)
     v1 = v0 + dt / 2.0 * (a0 + new_acc) + dt * dt / 12.0 * (j0 - new_jrk)
     x1 = x0 + dt / 2.0 * (v0 + v1) + dt * dt / 12.0 * (a0 - new_acc)
-    used = lax.broadcasted_iota(jnp.int32, (3, slots), 1) < count_ref[...]
-    state_ref[0:3] = jnp.where(used, x1, 0.0)
-    state_ref[3:6] = jnp.where(used, v1, 0.0)
-    deriv_ref[0:3] = jnp.where(used, new_acc, 0.0)
-    deriv_ref[3:6] = jnp.where(used, new_jrk, 0.0)
-
-    def sent(k, _):
+    used = lax.broadcasted_iota(jnp.int32, (3, slots), 1) < count_ref[0]
+    out_ref[0:3] = jnp.where(used, x1, 0.0)
+    out_ref[3:6] = jnp.where(used, v1, 0.0)
+    out_ref[8:11] = jnp.where(used, new_acc, 0.0)
+    out_ref[11:14] = jnp.where(used, new_jrk, 0.0)
+
+    def sent(k):
         copy_to(k).wait_send()
-        return 0
-
-    lax.fori_loop(1, n, sent, 0)
+
+    each(n, sent)
 
 
 def solution(mesh):
@@ -179,27 +215,32 @@
 
     def body(position, velocity, old_accel, old_jerk, mass, elapsed, active_index, active_count):
         width, slots = mass.shape[0], active_index.shape[0]
-        out = jax.ShapeDtypeStruct((6, slots), jnp.float32)
-        return pl.pallas_call(
+        args = (
+            position, velocity, old_accel, old_jerk,
+            mass[None, :], elapsed[None, :], active_index[None, :], active_count,
+        )
+        both = pl.pallas_call(
             functools.partial(kernel, n),
-            out_shape=(out, out),
-            in_specs=[pl.BlockSpec(memory_space=pltpu.VMEM)] * 8,
-            out_specs=(pl.BlockSpec(memory_space=pltpu.VMEM),) * 2,
-            scratch_shapes=[
+            out_shape=pltpu.VMEM((16, slots), jnp.float32),
+            in_specs=[pl.BlockSpec(memory_space=pltpu.HBM)] * len(args),
+            out_specs=pl.BlockSpec(memory_space=pltpu.VMEM),
+            scratch_shapes=[pltpu.VMEM(x.shape, x.dtype) for x in args[:-1]]
+            + [pltpu.SMEM((1,), jnp.int32)]
+            + [
                 pltpu.VMEM((n, 8, width), jnp.float32),
                 pltpu.VMEM((16, width), jnp.float32),
                 pltpu.VMEM((6, slots, LANES), jnp.float32),
                 pltpu.VMEM((6, slots, LANES), jnp.float32),
                 pltpu.SemaphoreType.DMA((n,)),
                 pltpu.SemaphoreType.DMA((n,)),
+                pltpu.SemaphoreType.DMA((len(args),)),
             ],
             compiler_params=pltpu.CompilerParams(
-                collective_id=0, has_side_effects=True, vmem_limit_bytes=16 << 20
+                collective_id=0, has_side_effects=True, vmem_limit_bytes=60 << 20
             ),
-        )(
-            position, velocity, old_accel, old_jerk,
-            mass[None, :], elapsed[None, :], active_index[None, :], active_count[None, :],
-        )
+            name="forces",
+        )(*args)
+        return both[0:6], both[8:14]
 
     wide, flat = P(None, ("groups", "col")), P(("groups", "col"))
     return jax.shard_map(

time: 20.7 us -> 16.6 us (0.80)
  local copies, waits for them, and re-layouts: 4.6 us -> 0.61 us
    unnamed x16 -> x0, local copies, waits for them, and re-layouts: 4.6 us -> none
    slice x0 -> x1, local copies, waits for them, and re-layouts: none -> 0.61 us  [body(): return (both[0:6], both[8:14])]
where the time goes in v2:
time: 16.6 us; the launch traced here: 16.4 us
  Pallas kernels  14.5 us (87%)
  between operations  1.29 us (8%)
  local copies, waits for them, and re-layouts  0.61 us (4%)
    pallas_call x1, Pallas kernels, body(): pl.pallas_call(functools.partial(kernel, n), out_shape=pltpu.VMEM((16, sl...  14.5 us
    slice x1, local copies, waits for them, and re-layouts, body(): return (both[0:6], both[8:14])  0.61 us

profile of v2, /device:TPU:0, one launch (start us, length us, event | category | flops | bytes accessed | tf_op | source)
XLA Modules:
  0.0 16.4 jit_solution(10230994176267129783)
XLA Ops:
  1.3 14.5 %forces.1 = f32[16,256]{1,0:T(8,128)S(1)} custom-call(f32[3,256]{1,0:T(4,128)} %pos_hbm.1, f32[3,256]{1,0:T(4,128)} %vel_hbm.1, f32[3,256]{1,0:T(4,128)} %acc_hbm.1, f32[3,256]{1,0:T(4,128)} %jrk_hbm.1, f32[1,256]{1,0:T(1,128)} %bitcast.3, f32[1,256]{1,0:T(1,128)} %bitcast.4, s32[1,256]{1,0:T(1,128)} %bitcast.5, s32[1]{0:T(128)S(6)} %copy.10.count_hbm), custom_call_target="tpu_custom_call" | custom-call | tf_op jit(solution)/shard_map/forces/pallas_call | solution.py:222
  15.8 0.6 %fusion = (f32[6,256]{1,0:T(8,128)}, f32[6,256]{1,0:T(8,128)}) fusion(f32[16,256]{1,0:T(8,128)S(1)} %forces.1), kind=kLoop, calls=%fused_computation | loop fusion | bytes 24576 | tf_op jit(solution)/shard_map/slice | solution.py:243

commit v3 on v2

--- a/solution.py
+++ b/solution.py
@@ -35,27 +35,16 @@
     return jnp.concatenate(outs, axis=1)
 
 
-def partner(me, k, n):
-    if n & (n - 1):
-        return lax.rem(me + k, n), lax.rem(me + n - k, n)
+def xor(me, k, n):
     other, bit = 0, 1
     while bit < n:
         other = other + lax.rem(lax.div(me, bit) + lax.div(jnp.int32(k), bit), 2) * bit
         bit *= 2
-    return other, other
-
-
-def each(n, step):
-    if n <= 32:
-        for k in range(1, n):
-            step(k)
-        return
-
-    def one(k, _):
-        step(k)
-        return 0
-
-    lax.fori_loop(1, n, one, 0)
+    return other
+
+
+def low_bit(k):
+    return k & -k
 
 
 def kernel(
@@ -84,13 +73,12 @@
 
     barrier = pltpu.get_barrier_semaphore()
 
-    def greet(k):
+    bits = [1 << i for i in range(n.bit_length() - 1)]
+    partners = [xor(me, bit, n) for bit in bits]
+    for peer in partners:
         pl.semaphore_signal(
-            barrier, inc=1, device_id={"col": partner(me, k, n)[0]},
-            device_id_type=pl.DeviceIdType.MESH,
-        )
-
-    each(n, greet)
+            barrier, inc=1, device_id={"col": peer}, device_id_type=pl.DeviceIdType.MESH
+        )
 
     for load in loads:
         load.wait()
@@ -102,23 +90,21 @@
     field[me, 6:7] = mass_ref[...]
     field[me, 7:8] = mass_ref[...]
 
-    pl.semaphore_wait(barrier, n - 1)
-
-    def copy_to(k):
-        peer = partner(me, k, n)[0]
+    pl.semaphore_wait(barrier, len(bits))
+
+    def hand_on(k, i):
+        b = xor(me, k, n)
         return pltpu.make_async_remote_copy(
-            src_ref=field.at[me],
-            dst_ref=field.at[me],
-            send_sem=send_sem.at[peer],
-            recv_sem=recv_sem.at[me],
-            device_id={"col": peer},
+            src_ref=field.at[b],
+            dst_ref=field.at[b],
+            send_sem=send_sem.at[k + bits[i]],
+            recv_sem=recv_sem.at[b],
+            device_id={"col": partners[i]},
             device_id_type=pl.DeviceIdType.MESH,
         )
 
-    def send(k):
-        copy_to(k).start()
-
-    each(n, send)
+    for i in reversed(range(len(bits))):
+        hand_on(0, i).start()
 
     raw[0:3] = pos_ref[...]
     raw[3:6] = vel_ref[...]
@@ -178,20 +164,29 @@
 
     add_block(me)
 
-    def arrive(k, _):
-        b = partner(me, k, n)[1]
+    order = sorted(range(1, n), key=lambda k: (k.bit_count(), k != 1, -low_bit(k), -k))
+
+    def arrive(step, _):
+        k = sum(jnp.where(step == i, offset, 0) for i, offset in enumerate(order))
+        b = xor(me, k, n)
         pltpu.make_async_remote_copy(
             src_ref=field.at[b],
             dst_ref=field.at[b],
-            send_sem=send_sem.at[b],
+            send_sem=send_sem.at[k],
             recv_sem=recv_sem.at[b],
-            device_id={"col": b},
+            device_id={"col": partners[0]},
             device_id_type=pl.DeviceIdType.MESH,
         ).wait_recv()
+        for i in reversed(range(len(bits) - 1)):
+
+            @pl.when(lax.rem(k, 2 * bits[i]) == 0)
+            def _():
+                hand_on(k, i).start()
+
         add_block(b)
         return 0
 
-    lax.fori_loop(1, n, arrive, 0)
+    lax.fori_loop(0, n - 1, arrive, 0)
 
     rows = [jnp.sum(total[c].T, axis=0, keepdims=True) for c in range(6)]
     new_acc = jnp.concatenate(rows[0:3], axis=0)
@@ -204,10 +199,9 @@
     out_ref[8:11] = jnp.where(used, new_acc, 0.0)
     out_ref[11:14] = jnp.where(used, new_jrk, 0.0)
 
-    def sent(k):
-        copy_to(k).wait_send()
-
-    each(n, sent)
+    for k in range(1, n):
+        bit = low_bit(k)
+        hand_on(k - bit, bits.index(bit)).wait_send()
 
 
 def solution(mesh):

time: 16.6 us -> 17.8 us (1.072)
  Pallas kernels: 14.5 us -> 15.7 us
    pallas_call x1, Pallas kernels: 14.5 us -> 15.7 us  [body(): pl.pallas_call(functools.partial(kernel, n), out_shape=pltpu.VMEM((16, sl...]
where the time goes in v3:
time: 17.8 us; the launch traced here: 17.6 us
  Pallas kernels  15.7 us (88%)
  between operations  1.29 us (7%)
  local copies, waits for them, and re-layouts  0.61 us (3%)
    pallas_call x1, Pallas kernels, body(): pl.pallas_call(functools.partial(kernel, n), out_shape=pltpu.VMEM((16, sl...  15.7 us
    slice x1, local copies, waits for them, and re-layouts, body(): return (both[0:6], both[8:14])  0.61 us

profile of v3, /device:TPU:0, one launch (start us, length us, event | category | flops | bytes accessed | tf_op | source)
XLA Modules:
  0.0 17.6 jit_solution(4420150846376854417)
XLA Ops:
  1.3 15.7 %forces.1 = f32[16,256]{1,0:T(8,128)S(1)} custom-call(f32[3,256]{1,0:T(4,128)} %pos_hbm.1, f32[3,256]{1,0:T(4,128)} %vel_hbm.1, f32[3,256]{1,0:T(4,128)} %acc_hbm.1, f32[3,256]{1,0:T(4,128)} %jrk_hbm.1, f32[1,256]{1,0:T(1,128)} %bitcast.3, f32[1,256]{1,0:T(1,128)} %bitcast.4, s32[1,256]{1,0:T(1,128)} %bitcast.5, s32[1]{0:T(128)S(6)} %copy.10.count_hbm), custom_call_target="tpu_custom_call" | custom-call | tf_op jit(solution)/shard_map/forces/pallas_call | solution.py:216
  17.0 0.6 %fusion = (f32[6,256]{1,0:T(8,128)}, f32[6,256]{1,0:T(8,128)}) fusion(f32[16,256]{1,0:T(8,128)S(1)} %forces.1), kind=kLoop, calls=%fused_computation | loop fusion | bytes 24576 | tf_op jit(solution)/shard_map/slice | solution.py:237

commit v4 on v3

--- a/solution.py
+++ b/solution.py
@@ -10,7 +10,7 @@
 soften_sq = 0.01
 LANES = 128
 SUBLANES = 8
-UNROLL = 16
+UNROLL = 32
 
 
 def predict(x, v, a, j, t):
@@ -41,10 +41,6 @@
         other = other + lax.rem(lax.div(me, bit) + lax.div(jnp.int32(k), bit), 2) * bit
         bit *= 2
     return other
-
-
-def low_bit(k):
-    return k & -k
 
 
 def kernel(
@@ -73,9 +69,9 @@
 
     barrier = pltpu.get_barrier_semaphore()
 
-    bits = [1 << i for i in range(n.bit_length() - 1)]
-    partners = [xor(me, bit, n) for bit in bits]
-    for peer in partners:
+    offsets = [1] + list(range(2, n, 2))
+    partners = {k: xor(me, k, n) for k in offsets}
+    for peer in partners.values():
         pl.semaphore_signal(
             barrier, inc=1, device_id={"col": peer}, device_id_type=pl.DeviceIdType.MESH
         )
@@ -90,21 +86,21 @@
     field[me, 6:7] = mass_ref[...]
     field[me, 7:8] = mass_ref[...]
 
-    pl.semaphore_wait(barrier, len(bits))
-
-    def hand_on(k, i):
+    pl.semaphore_wait(barrier, len(offsets))
+
+    def hand_on(k, offset):
         b = xor(me, k, n)
         return pltpu.make_async_remote_copy(
             src_ref=field.at[b],
             dst_ref=field.at[b],
-            send_sem=send_sem.at[k + bits[i]],
+            send_sem=send_sem.at[k + offset],
             recv_sem=recv_sem.at[b],
-            device_id={"col": partners[i]},
+            device_id={"col": partners[offset]},
             device_id_type=pl.DeviceIdType.MESH,
         )
 
-    for i in reversed(range(len(bits))):
-        hand_on(0, i).start()
+    for offset in offsets:
+        hand_on(0, offset).start()
 
     raw[0:3] = pos_ref[...]
     raw[3:6] = vel_ref[...]
@@ -164,7 +160,7 @@
 
     add_block(me)
 
-    order = sorted(range(1, n), key=lambda k: (k.bit_count(), k != 1, -low_bit(k), -k))
+    order = offsets + list(range(3, n, 2))
 
     def arrive(step, _):
         k = sum(jnp.where(step == i, offset, 0) for i, offset in enumerate(order))
@@ -174,14 +170,13 @@
             dst_ref=field.at[b],
             send_sem=send_sem.at[k],
             recv_sem=recv_sem.at[b],
-            device_id={"col": partners[0]},
+            device_id={"col": partners[1]},
             device_id_type=pl.DeviceIdType.MESH,
         ).wait_recv()
-        for i in reversed(range(len(bits) - 1)):
-
-            @pl.when(lax.rem(k, 2 * bits[i]) == 0)
-            def _():
-                hand_on(k, i).start()
+
+        @pl.when(lax.rem(k, 2) == 0)
+        def _():
+            hand_on(k, 1).start()
 
         add_block(b)
         return 0
@@ -199,9 +194,10 @@
     out_ref[8:11] = jnp.where(used, new_acc, 0.0)
     out_ref[11:14] = jnp.where(used, new_jrk, 0.0)
 
-    for k in range(1, n):
-        bit = low_bit(k)
-        hand_on(k - bit, bits.index(bit)).wait_send()
+    for offset in offsets:
+        hand_on(0, offset).wait_send()
+    for k in range(2, n, 2):
+        hand_on(k, 1).wait_send()
 
 
 def solution(mesh):

time: 17.8 us -> 16.7 us (0.938)
  Pallas kernels: 15.7 us -> 14.6 us
    pallas_call x1, Pallas kernels: 15.7 us -> 14.6 us  [body(): pl.pallas_call(functools.partial(kernel, n), out_shape=pltpu.VMEM((16, sl...]
where the time goes in v4:
time: 16.7 us; the launch traced here: 16.5 us
  Pallas kernels  14.6 us (87%)
  between operations  1.29 us (8%)
  local copies, waits for them, and re-layouts  0.61 us (4%)
    pallas_call x1, Pallas kernels, body(): pl.pallas_call(functools.partial(kernel, n), out_shape=pltpu.VMEM((16, sl...  14.6 us
    slice x1, local copies, waits for them, and re-layouts, body(): return (both[0:6], both[8:14])  0.61 us

profile of v4, /device:TPU:0, one launch (start us, length us, event | category | flops | bytes accessed | tf_op | source)
XLA Modules:
  0.0 16.5 jit_solution(13786493496238463739)
XLA Ops:
  1.3 14.6 %forces.1 = f32[16,256]{1,0:T(8,128)S(1)} custom-call(f32[3,256]{1,0:T(4,128)} %pos_hbm.1, f32[3,256]{1,0:T(4,128)} %vel_hbm.1, f32[3,256]{1,0:T(4,128)} %acc_hbm.1, f32[3,256]{1,0:T(4,128)} %jrk_hbm.1, f32[1,256]{1,0:T(1,128)} %bitcast.3, f32[1,256]{1,0:T(1,128)} %bitcast.4, s32[1,256]{1,0:T(1,128)} %bitcast.5, s32[1]{0:T(128)S(6)} %copy.10.count_hbm), custom_call_target="tpu_custom_call" | custom-call | tf_op jit(solution)/shard_map/forces/pallas_call | solution.py:212
  15.9 0.6 %fusion = (f32[6,256]{1,0:T(8,128)}, f32[6,256]{1,0:T(8,128)}) fusion(f32[16,256]{1,0:T(8,128)S(1)} %forces.1), kind=kLoop, calls=%fused_computation | loop fusion | bytes 24576 | tf_op jit(solution)/shard_map/slice | solution.py:233
